TPU v7x, 32 devices: a whole 2x2x4 slice. The times are simulated.
32 devices in a mesh: section: 4 (over y, x), patch: 2 (over core), chan: 4 (over z).
Axes of the slice: x: 2, y: 2, z: 4, core: 2. Of those that a mesh axis runs over, the one named last changes fastest.
Arguments:
- cond: bfloat16 [4, 128, 16, 128], P('section', 'chan', 'patch'), may hold values from -20 to 20
- noise: bfloat16 [4, 128, 16, 128], P('section', 'chan', 'patch'), may hold values from -6 to 6
- conv_weight: bfloat16 [4, 9, 128, 128], P('section', None, 'chan'), may hold values from -0.1875 to 0.1875
- mix_weight: bfloat16 [4, 128, 128], P('section', 'chan'), may hold values from -0.5 to 0.5
- norm_gain: float32 [4, 128], P('section', 'chan'), may hold values from 0.1 to 1.9
- norm_bias: float32 [4, 128], P('section', 'chan'), may hold values from -3 to 3
Outputs:
- field: bfloat16 [4, 128, 16, 128], P('section', 'chan', 'patch')
All inputs are finite; a program needn't handle non-finite values.
Results may differ from a plain program's by a relative error of at most 0.012.
Values may be sent and summed in bfloat16 or wider, within the bound.
A program may use at most 64 MiB of HBM per device.

v0:
```python
import jax
import jax.numpy as jnp
from jax import lax
from jax.sharding import PartitionSpec as P

C = 128
GROUPS = 32


def with_halo(cells, sides, width):
    for axis, dim in sides:
        count = lax.axis_size(axis)
        ends = count - 1
        head = lax.slice_in_dim(cells, 0, width, axis=dim)
        tail = lax.slice_in_dim(cells, cells.shape[dim] - width, cells.shape[dim], axis=dim)
        cells = jnp.concatenate(
            [
                lax.ppermute(tail, axis, [(i, (i + 1) % count) for i in range(ends)]),
                cells,
                lax.ppermute(head, axis, [((i + 1) % count, i) for i in range(ends)]),
            ],
            axis=dim,
        )
    return cells


def from_root(value, axis, source):
    kept = jnp.where(lax.axis_index(axis) == source, value, 0).astype(value.dtype)
    return lax.psum(kept, axis)


def conv_taps(running, row_padded, tap_weight, num_rows, num_cols):
    padded = jnp.pad(row_padded, ((0, 0), (0, 0), (0, 0), (1, 1)))
    for tap_index in range(9):
        row_off, col_off = divmod(tap_index, 3)
        window = padded[:, :, row_off : row_off + num_rows, col_off : col_off + num_cols]
        running = running + jnp.einsum(
            "oc,bchw->bohw", tap_weight[tap_index], window, preferred_element_type=jnp.float32
        )
    return running


def group_norm(conv_total, gain_row, bias_row):
    batch_size, out_chans, num_rows, num_cols = conv_total.shape
    group_size = C // GROUPS
    grouped = conv_total.reshape(
        batch_size, out_chans // group_size, group_size, num_rows, num_cols
    )
    local_sums = jnp.sum(grouped, axis=(2, 3, 4))
    local_squares = jnp.sum(grouped * grouped, axis=(2, 3, 4))
    sums, squares = lax.psum((local_sums, local_squares), "patch")
    entries = group_size * num_rows * num_cols * lax.axis_size("patch")
    group_mean = sums / entries
    variance = squares / entries - group_mean * group_mean
    scale_now = 1.0 / jnp.sqrt(variance + 1e-05)
    normed = (grouped - group_mean[:, :, None, None, None]) * scale_now[:, :, None, None, None]
    normed = normed.reshape(batch_size, out_chans, num_rows, num_cols)
    normed = normed * gain_row[None, :, None, None] + bias_row[None, :, None, None]
    return jax.nn.silu(normed).astype(jnp.bfloat16)


def apply_block(inputs, params):
    tap_weight, mix_matrix, gain_row, bias_row = params
    batch_size = inputs.shape[0]
    num_rows = inputs.shape[2]
    num_cols = inputs.shape[3]
    out_chans = tap_weight.shape[1]
    padded = with_halo(inputs, (("patch", 2),), 1)
    empty = jnp.zeros((batch_size, out_chans, num_rows, num_cols), jnp.float32)
    weight_part = tap_weight
    conv_total = conv_taps(
        empty, lax.all_gather(padded, "chan", axis=1, tiled=True), weight_part, num_rows, num_cols
    )
    acted = group_norm(conv_total, gain_row, bias_row)
    weight_part = mix_matrix
    return jnp.einsum(
        "oc,bchw->bohw",
        weight_part,
        lax.all_gather(acted, "chan", axis=1, tiled=True),
        preferred_element_type=jnp.float32,
    )


def prepare(params):
    tap_weight = params[0][0]
    mix_matrix = params[1][0]
    gain_row = params[2][0]
    bias_row = params[3][0]
    return (tap_weight, mix_matrix, gain_row, bias_row)


def body(cond, noise, conv_weight, mix_weight, norm_gain, norm_bias):
    sections = lax.axis_size("section")
    mean_field = cond
    sample = noise
    for layer_index in range(sections):
        shared = (
            from_root(conv_weight, "section", layer_index),
            from_root(mix_weight, "section", layer_index),
            from_root(norm_gain.astype(jnp.bfloat16), "section", layer_index).astype(
                norm_gain.dtype
            ),
            from_root(norm_bias.astype(jnp.bfloat16), "section", layer_index).astype(
                norm_bias.dtype
            ),
        )
        params = prepare(shared)
        if layer_index == 0:
            first_out = apply_block(cond, params)
            mean_field = (cond.astype(jnp.float32) + first_out).astype(jnp.bfloat16)
        else:
            inputs = (sample.astype(jnp.float32) + mean_field.astype(jnp.float32)).astype(
                jnp.bfloat16
            )
            denoised = apply_block(inputs, params)
            before = sample.astype(jnp.float32)
            sample = (before + 0.5 * (denoised - before)).astype(jnp.bfloat16)
    result = (sample.astype(jnp.float32) + mean_field.astype(jnp.float32)).astype(jnp.bfloat16)
    return result


def solution(mesh):
    return jax.shard_map(
        body,
        mesh=mesh,
        in_specs=(
            P("section", "chan", "patch", None),
            P("section", "chan", "patch", None),
            P("section", None, "chan", None),
            P("section", "chan", None),
            P("section", "chan"),
            P("section", "chan"),
        ),
        out_specs=P("section", "chan", "patch", None),
        check_vma=False,
    )
```

profile of v0, /device:TPU:0, one launch (start us, length us, event | category | flops | bytes accessed | tf_op | source)
XLA Modules:
  0.0 206.2 jit_solution(15433251805935275792)
XLA Ops:
  6.5 0.9 copy.14
  7.4 2.4 %collective-permute-start = (bf16[1,32,1,128]{3,1,2,0:T(8,128)(2,1)S(1)}, bf16[1,32,1,128]{3,1,2,0:T(8,128)(2,1)S(1)}, u32[]{:S(2)}, u32[]{:S(2)}) collective-permute-start(bf16[1,32,1,128]{3,1,2,0:T(8,128)(2,1)S(1)} %get-tuple-element.39), channel_id=1, source_target_pairs={{0,4},{1,5},{2,6},{3,7},{8,12},{9,13},{10,14},{11,15},{16,20},{17,... | collective-permute-start | bytes 24584 | tf_op jit(solution)/shard_map/ppermute | solution.py:18
  9.8 1.3 collective-permute-start.1
  11.1 0.7 broadcast_select_fusion
  11.9 0.7 copy-done.7
  12.6 0.6 copy-done.8
  13.2 17.7 %all-reduce.8 = (bf16[32]{0:T(256)(128)(2,1)S(1)}, bf16[32]{0:T(256)(128)(2,1)S(1)}, bf16[32,128]{1,0:T(8,128)(2,1)S(1)}, bf16[32]{0:T(256)(128)(2,1)S(1)}, bf16...) all-reduce(bf16[32]{0:T(256)(128)(2,1)S(1)} %get-tuple-element.75, ...), channel_id=1, replica_groups=mesh['section'=4,'patch'=2,'chan'=4] {'section'}, use_global_device_ids=true, to_apply=%region_8.9 | all-reduce | flops 16640 | bytes 66560 | tf_op jit(solution)/shard_map/psum | solution.py:29
  31.0 15.1 %all_gather.24 = bf16[1,128,10,128]{3,1,2,0:T(8,128)(2,1)S(1)} all-gather(bf16[1,32,10,128]{3,1,2,0:T(8,128)(2,1)S(1)} %pad_maximum_fusion), channel_id=1, replica_groups=mesh['section'=4,'patch'=2,'chan'=4] {'chan'}, dimensions={1}, use_global_device_ids=true | all-gather | bytes 409600 | tf_op jit(solution)/shard_map/all_gather | solution.py:72
  46.1 13.0 %all-reduce.12.cloned.1.call-done = (bf16[1,9,32,128]{3,2,1,0:T(8,128)(2,1)}, bf16[1,9,32,128]{3,2,1,0:T(8,128)(2,1)}, bf16[1,9,32,128]{3,2,1,0:T(8,128)(2,1)}, bf16[1,9,32,128]{3,2,1,0:T(8,128)(2,1)}) async-done(((bf16[1,9,32,128]{3,2,1,0:T(8,128)(2,1)}, bf16[1,9,32,128]{3,2,1,0:T(8,128)(2,1)}, bf16[1,9,32,128]{3,2,1,0:T(8,128)(2,1)}, bf16[1,9,32,128]{3,2,1,0:T(8,128)(2,1)}), ...) | async-done | bytes 294928 | tf_op jit(solution)/shard_map/psum | solution.py:29
  59.0 1.0 fusion.21
  60.1 0.2 convolution_add_fusion.31
  60.2 0.3 convolution_add_fusion.30
  60.5 0.3 convolution_add_fusion.29
  60.8 0.2 convolution_add_fusion.28
  60.9 0.3 convolution_add_fusion.27
  61.2 0.3 convolution_add_fusion.26
  61.5 0.2 convolution_add_fusion.25
  61.7 0.4 fusion.101
  62.6 2.5 %all-reduce.7 = (f32[1,8]{1,0:T(1,128)S(1)}, f32[1,8]{1,0:T(1,128)S(1)}) all-reduce(f32[1,8]{1,0:T(1,128)S(1)} %bitcast.561, f32[1,8]{1,0:T(1,128)S(1)} %bitcast.557), channel_id=1, replica_groups=mesh['section'=4,'patch'=2,'chan'=4] {'patch'}, use_global_device_ids=true, to_apply=%region_6.7 | all-reduce | flops 16 | bytes 128 | tf_op jit(solution)/shard_map/psum | solution.py:51
  65.5 14.1 %all_gather.25 = bf16[1,128,8,128]{3,1,2,0:T(8,128)(2,1)S(1)} all-gather(bf16[1,32,8,128]{3,1,2,0:T(8,128)(2,1)S(1)} %fusion.105), channel_id=1, replica_groups=mesh['section'=4,'patch'=2,'chan'=4] {'chan'}, dimensions={1}, use_global_device_ids=true | all-gather | bytes 327680 | tf_op jit(solution)/shard_map/all_gather | solution.py:79
  79.6 0.2 fusion.76
  79.8 1.3 collective-permute-start.2
  81.1 1.3 collective-permute-start.3
  82.4 1.7 collective-permute-done.3
  84.2 14.7 %all_gather.26 = bf16[1,128,10,128]{3,1,2,0:T(8,128)(2,1)S(1)} all-gather(bf16[1,32,10,128]{3,1,2,0:T(8,128)(2,1)S(1)} %pad_maximum_fusion.1), channel_id=1, replica_groups=mesh['section'=4,'patch'=2,'chan'=4] {'chan'}, dimensions={1}, use_global_device_ids=true | all-gather | bytes 409600 | tf_op jit(solution)/shard_map/all_gather | solution.py:72
  98.9 0.3 fusion.34
  99.1 0.2 convolution_add_fusion.23
  99.3 0.3 convolution_add_fusion.22
  99.6 0.3 convolution_add_fusion.21
  100.0 0.3 convolution_add_fusion.19
  100.3 0.3 convolution_add_fusion.18
  100.7 0.4 fusion.94
  101.7 2.5 %all-reduce.6 = (f32[1,8]{1,0:T(1,128)S(1)}, f32[1,8]{1,0:T(1,128)S(1)}) all-reduce(f32[1,8]{1,0:T(1,128)S(1)} %bitcast.562, f32[1,8]{1,0:T(1,128)S(1)} %bitcast.558), channel_id=1, replica_groups=mesh['section'=4,'patch'=2,'chan'=4] {'patch'}, use_global_device_ids=true, to_apply=%region_16.17 | all-reduce | flops 16 | bytes 128 | tf_op jit(solution)/shard_map/psum | solution.py:51
  104.6 14.4 %all_gather.27 = bf16[1,128,8,128]{3,1,2,0:T(8,128)(2,1)S(1)} all-gather(bf16[1,32,8,128]{3,1,2,0:T(8,128)(2,1)S(1)} %fusion.106), channel_id=1, replica_groups=mesh['section'=4,'patch'=2,'chan'=4] {'chan'}, dimensions={1}, use_global_device_ids=true | all-gather | bytes 327680 | tf_op jit(solution)/shard_map/all_gather | solution.py:79
  119.0 0.2 add_convert_fusion.1
  119.2 1.3 collective-permute-start.4
  120.5 1.3 collective-permute-start.5
  121.8 1.7 collective-permute-done.5
  123.6 15.0 %all_gather.28 = bf16[1,128,10,128]{3,1,2,0:T(8,128)(2,1)S(1)} all-gather(bf16[1,32,10,128]{3,1,2,0:T(8,128)(2,1)S(1)} %pad_maximum_fusion.2), channel_id=1, replica_groups=mesh['section'=4,'patch'=2,'chan'=4] {'chan'}, dimensions={1}, use_global_device_ids=true | all-gather | bytes 409600 | tf_op jit(solution)/shard_map/all_gather | solution.py:72
  138.6 0.3 fusion.47
  139.0 0.3 convolution_add_fusion.14
  139.3 0.3 convolution_add_fusion.13
  139.6 0.2 convolution_add_fusion.12
  139.8 0.3 convolution_add_fusion.11
  140.0 0.3 convolution_add_fusion.10
  140.5 0.4 fusion.87
  141.4 2.5 %all-reduce.5 = (f32[1,8]{1,0:T(1,128)S(1)}, f32[1,8]{1,0:T(1,128)S(1)}) all-reduce(f32[1,8]{1,0:T(1,128)S(1)} %bitcast.563, f32[1,8]{1,0:T(1,128)S(1)} %bitcast.559), channel_id=1, replica_groups=mesh['section'=4,'patch'=2,'chan'=4] {'patch'}, use_global_device_ids=true, to_apply=%region_26.27 | all-reduce | flops 16 | bytes 128 | tf_op jit(solution)/shard_map/psum | solution.py:51
  144.3 14.4 %all_gather.29 = bf16[1,128,8,128]{3,1,2,0:T(8,128)(2,1)S(1)} all-gather(bf16[1,32,8,128]{3,1,2,0:T(8,128)(2,1)S(1)} %fusion.107), channel_id=1, replica_groups=mesh['section'=4,'patch'=2,'chan'=4] {'chan'}, dimensions={1}, use_global_device_ids=true | all-gather | bytes 327680 | tf_op jit(solution)/shard_map/all_gather | solution.py:79
  158.7 0.2 add_convert_fusion
  158.9 1.3 collective-permute-start.6
  160.2 1.3 collective-permute-start.7
  161.6 1.7 collective-permute-done.7
  163.3 15.0 %all_gather.30 = bf16[1,128,10,128]{3,1,2,0:T(8,128)(2,1)S(1)} all-gather(bf16[1,32,10,128]{3,1,2,0:T(8,128)(2,1)S(1)} %pad_maximum_fusion.3), channel_id=1, replica_groups=mesh['section'=4,'patch'=2,'chan'=4] {'chan'}, dimensions={1}, use_global_device_ids=true | all-gather | bytes 409600 | tf_op jit(solution)/shard_map/all_gather | solution.py:72
  178.4 0.3 fusion.60
  178.8 0.3 convolution_add_fusion.6
  179.1 0.3 convolution_add_fusion.5
  179.3 0.2 convolution_add_fusion.4
  179.5 0.3 convolution_add_fusion.3
  179.8 0.3 convolution_add_fusion.2
  180.2 0.4 fusion.80
  181.1 2.5 %all-reduce.4 = (f32[1,8]{1,0:T(1,128)S(1)}, f32[1,8]{1,0:T(1,128)S(1)}) all-reduce(f32[1,8]{1,0:T(1,128)S(1)} %bitcast.560, f32[1,8]{1,0:T(1,128)S(1)} %bitcast.556), channel_id=1, replica_groups=mesh['section'=4,'patch'=2,'chan'=4] {'patch'}, use_global_device_ids=true, to_apply=%region_36.37 | all-reduce | flops 16 | bytes 128 | tf_op jit(solution)/shard_map/psum | solution.py:51
  184.1 14.4 %all_gather.31 = bf16[1,128,8,128]{3,1,2,0:T(8,128)(2,1)S(1)} all-gather(bf16[1,32,8,128]{3,1,2,0:T(8,128)(2,1)S(1)} %fusion.108), channel_id=1, replica_groups=mesh['section'=4,'patch'=2,'chan'=4] {'chan'}, dimensions={1}, use_global_device_ids=true | all-gather | bytes 327680 | tf_op jit(solution)/shard_map/all_gather | solution.py:79
  198.5 0.2 fusion.16
  198.7 0.7 copy.18
  (93 shorter events, 5.0 us)
Async XLA Ops:
  6.5 4.6 %copy-start.6 = (bf16[1,9,32,128]{3,2,1,0:T(8,128)(2,1)S(1)}, bf16[1,9,32,128]{3,2,1,0:T(8,128)(2,1)}, u32[]{:S(2)}) copy-start(bf16[1,9,32,128]{3,2,1,0:T(8,128)(2,1)} %param.8) | copy-start | bytes 221188
  6.5 52.5 %all-reduce.12.cloned.1.call-start = ((), (), s32[]{:S(2)}) async-start(), calls=%async_computation | async-start | bytes 589824 | tf_op jit(solution)/shard_map/psum | solution.py:29
  7.4 23.5 %collective-permute-start = (bf16[1,32,1,128]{3,1,2,0:T(8,128)(2,1)S(1)}, bf16[1,32,1,128]{3,1,2,0:T(8,128)(2,1)S(1)}, u32[]{:S(2)}, u32[]{:S(2)}) collective-permute-start(bf16[1,32,1,128]{3,1,2,0:T(8,128)(2,1)S(1)} %get-tuple-element.39), channel_id=1, source_target_pairs={{0,4},{1,5},{2,6},{3,7},{8,12},{9,13},{10,14},{11,15},{16,20},{17,... | collective-permute-start | bytes 24584 | tf_op jit(solution)/shard_map/ppermute | solution.py:18
  9.8 21.2 %collective-permute-start.1 = (bf16[1,32,1,128]{3,1,2,0:T(8,128)(2,1)S(1)}, bf16[1,32,1,128]{3,1,2,0:T(8,128)(2,1)S(1)}, u32[]{:S(2)}, u32[]{:S(2)}) collective-permute-start(bf16[1,32,1,128]{3,1,2,0:T(8,128)(2,1)S(1)} %get-tuple-element.40), channel_id=1, source_target_pairs={{4,0},{5,1},{6,2},{7,3},{12,8},{13,9},{14,10},{15,11},{20,16},{21,... | collective-permute-start | bytes 24584 | tf_op jit(solution)/shard_map/ppermute | solution.py:20
  11.8 0.7 copy-start.7
  12.5 0.7 copy-start.8
  12.5 0.7 copy-start.9
  59.0 1.0 copy-start.5
  65.5 14.1 %copy-start = (bf16[1,32,8,128]{3,2,1,0:T(8,128)(2,1)S(1)}, bf16[1,32,8,128]{3,2,1,0:T(8,128)(2,1)}, u32[]{:S(2)}) copy-start(bf16[1,32,8,128]{3,2,1,0:T(8,128)(2,1)} %param.6) | copy-start | bytes 196612
  65.5 14.1 %copy-start.1 = (bf16[1,32,8,128]{3,2,1,0:T(8,128)(2,1)S(1)}, bf16[1,32,8,128]{3,2,1,0:T(8,128)(2,1)}, u32[]{:S(2)}) copy-start(bf16[1,32,8,128]{3,2,1,0:T(8,128)(2,1)} %param.7) | copy-start | bytes 196612
  79.8 2.6 %collective-permute-start.2 = (bf16[1,32,1,128]{3,1,2,0:T(8,128)(2,1)S(1)}, bf16[1,32,1,128]{3,1,2,0:T(8,128)(2,1)S(1)}, u32[]{:S(2)}, u32[]{:S(2)}) collective-permute-start(bf16[1,32,1,128]{3,1,2,0:T(8,128)(2,1)S(1)} %get-tuple-element.37), channel_id=1, source_target_pairs={{0,4},{1,5},{2,6},{3,7},{8,12},{9,13},{10,14},{11,15},{16,20},{17,... | collective-permute-start | bytes 24584 | tf_op jit(solution)/shard_map/ppermute | solution.py:18
  81.1 3.1 %collective-permute-start.3 = (bf16[1,32,1,128]{3,1,2,0:T(8,128)(2,1)S(1)}, bf16[1,32,1,128]{3,1,2,0:T(8,128)(2,1)S(1)}, u32[]{:S(2)}, u32[]{:S(2)}) collective-permute-start(bf16[1,32,1,128]{3,1,2,0:T(8,128)(2,1)S(1)} %get-tuple-element.38), channel_id=1, source_target_pairs={{4,0},{5,1},{6,2},{7,3},{12,8},{13,9},{14,10},{15,11},{20,16},{21,... | collective-permute-start | bytes 24584 | tf_op jit(solution)/shard_map/ppermute | solution.py:20
  84.2 14.7 %copy-start.4 = (bf16[1,9,32,128]{3,2,1,0:T(8,128)(2,1)S(1)}, bf16[1,9,32,128]{3,2,1,0:T(8,128)(2,1)}, u32[]{:S(2)}) copy-start(bf16[1,9,32,128]{3,2,1,0:T(8,128)(2,1)} %get-tuple-element.26) | copy-start | bytes 221188
  119.2 2.6 %collective-permute-start.4 = (bf16[1,32,1,128]{3,1,2,0:T(8,128)(2,1)S(1)}, bf16[1,32,1,128]{3,1,2,0:T(8,128)(2,1)S(1)}, u32[]{:S(2)}, u32[]{:S(2)}) collective-permute-start(bf16[1,32,1,128]{3,1,2,0:T(8,128)(2,1)S(1)} %get-tuple-element.35), channel_id=1, source_target_pairs={{0,4},{1,5},{2,6},{3,7},{8,12},{9,13},{10,14},{11,15},{16,20},{17,... | collective-permute-start | bytes 24584 | tf_op jit(solution)/shard_map/ppermute | solution.py:18
  120.5 3.1 %collective-permute-start.5 = (bf16[1,32,1,128]{3,1,2,0:T(8,128)(2,1)S(1)}, bf16[1,32,1,128]{3,1,2,0:T(8,128)(2,1)S(1)}, u32[]{:S(2)}, u32[]{:S(2)}) collective-permute-start(bf16[1,32,1,128]{3,1,2,0:T(8,128)(2,1)S(1)} %get-tuple-element.36), channel_id=1, source_target_pairs={{4,0},{5,1},{6,2},{7,3},{12,8},{13,9},{14,10},{15,11},{20,16},{21,... | collective-permute-start | bytes 24584 | tf_op jit(solution)/shard_map/ppermute | solution.py:20
  123.6 15.0 %copy-start.3 = (bf16[1,9,32,128]{3,2,1,0:T(8,128)(2,1)S(1)}, bf16[1,9,32,128]{3,2,1,0:T(8,128)(2,1)}, u32[]{:S(2)}) copy-start(bf16[1,9,32,128]{3,2,1,0:T(8,128)(2,1)} %get-tuple-element.27) | copy-start | bytes 221188
  158.9 2.6 %collective-permute-start.6 = (bf16[1,32,1,128]{3,1,2,0:T(8,128)(2,1)S(1)}, bf16[1,32,1,128]{3,1,2,0:T(8,128)(2,1)S(1)}, u32[]{:S(2)}, u32[]{:S(2)}) collective-permute-start(bf16[1,32,1,128]{3,1,2,0:T(8,128)(2,1)S(1)} %get-tuple-element.33), channel_id=1, source_target_pairs={{0,4},{1,5},{2,6},{3,7},{8,12},{9,13},{10,14},{11,15},{16,20},{17,... | collective-permute-start | bytes 24584 | tf_op jit(solution)/shard_map/ppermute | solution.py:18
  160.2 3.1 %collective-permute-start.7 = (bf16[1,32,1,128]{3,1,2,0:T(8,128)(2,1)S(1)}, bf16[1,32,1,128]{3,1,2,0:T(8,128)(2,1)S(1)}, u32[]{:S(2)}, u32[]{:S(2)}) collective-permute-start(bf16[1,32,1,128]{3,1,2,0:T(8,128)(2,1)S(1)} %get-tuple-element.34), channel_id=1, source_target_pairs={{4,0},{5,1},{6,2},{7,3},{12,8},{13,9},{14,10},{15,11},{20,16},{21,... | collective-permute-start | bytes 24584 | tf_op jit(solution)/shard_map/ppermute | solution.py:20
  163.3 15.0 %copy-start.2 = (bf16[1,9,32,128]{3,2,1,0:T(8,128)(2,1)S(1)}, bf16[1,9,32,128]{3,2,1,0:T(8,128)(2,1)}, u32[]{:S(2)}) copy-start(bf16[1,9,32,128]{3,2,1,0:T(8,128)(2,1)} %get-tuple-element.28) | copy-start | bytes 221188
Sparse Core Ops, SparseCore 0:
  12.0 46.9 all-reduce.11
where the time goes:
time: 207 us; the launch traced here: 206 us
  blocking collectives  145 us (70%)
  waiting for transfers between devices  18.2 us (9%)
  between operations  13.9 us (7%)
  starting transfers between devices  11.4 us (6%)
  matrix products  10.4 us (5%)
  local copies, waits for them, and re-layouts  4.77 us (2%)
  other arithmetic  2.86 us (1%)
    all_gather x4, blocking collectives, apply_block(): lax.all_gather(padded, 'chan', axis=1, tiled=True)  59.8 us
    all_gather x4, blocking collectives, apply_block(): lax.all_gather(acted, 'chan', axis=1, tiled=True)  57.3 us
    psum x1, blocking collectives, from_root(): return lax.psum(kept, axis)  17.7 us
    psum x1, waiting for transfers between devices, from_root(): return lax.psum(kept, axis)  13 us
    psum x4, blocking collectives, group_norm(): sums, squares = lax.psum((local_sums, local_squares), 'patch')  9.88 us
    dot_general x36, matrix products, conv_taps(): jnp.einsum('oc,bchw->bohw', tap_weight[tap_index], window, preferred_elem...  9.68 us
    ppermute x4, starting transfers between devices, with_halo(): lax.ppermute(tail, axis, [(i, (i + 1) % count) for i in range(ends)])  6.23 us
    ppermute x4, waiting for transfers between devices, with_halo(): lax.ppermute(head, axis, [((i + 1) % count, i) for i in range(ends)])  5.2 us
  transfers between devices with their start and end apart: 9, of which 4 were waited for; matrix products, arithmetic and copies ran while one was open for 0% of the time, Pallas kernels for 0%

commit v1 on v0

--- a/solution.py
+++ b/solution.py
@@ -1,6 +1,10 @@
+import functools
+
 import jax
 import jax.numpy as jnp
 from jax import lax
+from jax.experimental import pallas as pl
+from jax.experimental.pallas import tpu as pltpu
 from jax.sharding import PartitionSpec as P
 
 C = 128
@@ -119,9 +123,315 @@
     return result
 
 
+MESH = pl.DeviceIdType.MESH
+AXES = ("section", "patch", "chan")
+
+
+def remote(src, dst, send_sem, recv_sem, section, patch, chan):
+    return pltpu.make_async_remote_copy(
+        src_ref=src,
+        dst_ref=dst,
+        send_sem=send_sem,
+        recv_sem=recv_sem,
+        device_id=(section, patch, chan),
+        device_id_type=MESH,
+    )
+
+
+def whole_kernel(
+    sections, chans, rows, cols,
+    cond_in, noise_in, conv_in, mix_in, gb_in, out_ref,
+    cond_f, noise_f, mean_f, weights, gb, shifted, conv_f,
+    load_sem, wz_send, wz_recv, ws_send, ws_recv, wc_send, wc_recv,
+    gz_send, gz_recv, gs_send, gs_recv,
+    cz_send, cz_recv, cc_send, cc_recv, nz_send, nz_recv, nc_send, nc_recv,
+):
+    s = lax.axis_index("section")
+    p = lax.axis_index("patch")
+    z = lax.axis_index("chan")
+    other = 1 - p
+    taps = 10
+    half = taps // 2
+    part = C // chans
+    cells = rows * cols
+    sec_peers = [lax.rem(s + d, sections) for d in range(1, sections)]
+    z_peers = [lax.rem(z + d, chans) for d in range(1, chans)]
+
+    def band(index):
+        return pl.ds(pl.multiple_of(index * part, part), part)
+
+    mine = band(z)
+    loads = [
+        pltpu.make_async_copy(
+            conv_in.at[pl.ds(p * half, half - 1)],
+            weights.at[s, pl.ds(p * half, half - 1), mine, :],
+            load_sem.at[0],
+        ),
+        pltpu.make_async_copy(gb_in, gb.at[s, z], load_sem.at[2]),
+        pltpu.make_async_copy(cond_in, cond_f.at[p, mine, :], load_sem.at[3]),
+        pltpu.make_async_copy(noise_in, noise_f.at[p, mine, :], load_sem.at[4]),
+    ]
+    for copy in loads:
+        copy.start()
+    fifth = weights.at[s, p * half + half - 1, mine, :]
+
+    @pl.when(p == 0)
+    def _():
+        pltpu.make_async_copy(conv_in.at[half - 1], fifth, load_sem.at[1]).start()
+
+    @pl.when(p != 0)
+    def _():
+        pltpu.make_async_copy(mix_in, fifth, load_sem.at[1]).start()
+
+    barrier = pltpu.get_barrier_semaphore()
+    for peer in sec_peers:
+        pl.semaphore_signal(barrier, inc=1, device_id=(peer, p, z), device_id_type=MESH)
+    for peer in z_peers:
+        pl.semaphore_signal(barrier, inc=1, device_id=(s, p, peer), device_id_type=MESH)
+    pl.semaphore_signal(barrier, inc=1, device_id=(s, other, z), device_id_type=MESH)
+    pl.semaphore_wait(barrier, sections + chans - 1)
+
+    def w_half(layer, which):
+        return weights.at[layer, pl.ds(which * half, half)]
+
+    def w_shard(owner):
+        return weights.at[s, pl.ds(p * half, half), band(owner), :]
+
+    def w_z(d, owner):
+        return remote(w_shard(owner), w_shard(owner), wz_send.at[d], wz_recv.at[owner], s, p, z_peers[d])
+
+    def g_z(d, owner):
+        return remote(gb.at[s, owner], gb.at[s, owner], gz_send.at[d], gz_recv.at[owner], s, p, z_peers[d])
+
+    def w_s(d, layer):
+        return remote(w_half(layer, p), w_half(layer, p), ws_send.at[d], ws_recv.at[layer], sec_peers[d], p, z)
+
+    def g_s(d, layer):
+        return remote(gb.at[layer], gb.at[layer], gs_send.at[d], gs_recv.at[layer], sec_peers[d], p, z)
+
+    def w_c(layer, which):
+        return remote(w_half(layer, which), w_half(layer, which), wc_send.at[layer], wc_recv.at[layer], s, other, z)
+
+    def f_z(field, send, recv, d, owner):
+        block = field.at[p, band(owner), :]
+        return remote(block, block, send.at[d], recv.at[owner], s, p, z_peers[d])
+
+    def f_c(field, send, recv, which, owner):
+        block = field.at[which, band(owner), :]
+        return remote(block, block, send.at[owner], recv.at[owner], s, other, z)
+
+    steps = range(chans - 1)
+    for copy in loads[:2]:
+        copy.wait()
+    pltpu.make_async_copy(mix_in, fifth, load_sem.at[1]).wait()
+    for d in steps:
+        w_z(d, z).start()
+        g_z(d, z).start()
+    loads[2].wait()
+    for d in steps:
+        f_z(cond_f, cz_send, cz_recv, d, z).start()
+    f_c(cond_f, cc_send, cc_recv, p, z).start()
+    loads[3].wait()
+
+    zero_row = jnp.zeros((3 * C, cols), jnp.bfloat16)
+    shifted[:, 0:cols] = zero_row
+    shifted[:, (rows + 1) * cols : (rows + 2) * cols] = zero_row
+
+    for d in steps:
+        w_z(d, z_peers[d]).wait_recv()
+        g_z(d, z_peers[d]).wait_recv()
+    for d in range(sections - 1):
+        w_s(d, s).start()
+        g_s(d, s).start()
+    w_c(s, p).start()
+    for d in steps:
+        f_z(noise_f, nz_send, nz_recv, d, z).start()
+    f_c(noise_f, nc_send, nc_recv, p, z).start()
+
+    def forward_field(field, z_send, z_recv, c_send, c_recv):
+        for d in steps:
+            f_z(field, z_send, z_recv, d, z_peers[d]).wait_recv()
+            f_c(field, c_send, c_recv, p, z_peers[d]).start()
+        for owner in range(chans):
+            f_c(field, c_send, c_recv, other, owner).wait_recv()
+
+    def forward_layer(layer):
+        @pl.when(s != layer)
+        def _():
+            w_s(0, layer).wait_recv()
+            g_s(0, layer).wait_recv()
+            w_c(layer, p).start()
+
+    lane = lax.broadcasted_iota(jnp.int32, (C, cols), 1)
+    chan_row = lax.broadcasted_iota(jnp.int32, (C, cols), 0)
+    per_patch = rows // 2
+
+    def put_row(values, row):
+        base = (row + 1) * cols
+        left = jnp.where(lane == 0, 0.0, pltpu.roll(values, 1, 1))
+        right = jnp.where(lane == cols - 1, 0.0, pltpu.roll(values, cols - 1, 1))
+        shifted[0:C, pl.ds(base, cols)] = left.astype(jnp.bfloat16)
+        shifted[C : 2 * C, pl.ds(base, cols)] = values.astype(jnp.bfloat16)
+        shifted[2 * C : 3 * C, pl.ds(base, cols)] = right.astype(jnp.bfloat16)
+
+    def group_sum(values):
+        total = jnp.broadcast_to(jnp.sum(values, axis=1, keepdims=True), (C, cols))
+        for bit in (1, 2):
+            pair = jnp.where(
+                (chan_row // bit) % 2 == 0, pltpu.roll(total, C - bit, 0), pltpu.roll(total, bit, 0)
+            )
+            total = total + pair
+        return total
+
+    chunk_rows = 4
+    chunk = chunk_rows * cols
+    per_half = per_patch // chunk_rows
+
+    def conv_and_stats(layer):
+        lhs = jnp.concatenate([weights[layer, tap] for tap in range(9)], axis=1)
+        sums = jnp.zeros((C, cols), jnp.float32)
+        squares = jnp.zeros((C, cols), jnp.float32)
+        for q in range(rows // chunk_rows):
+            rhs = jnp.concatenate(
+                [shifted[:, q * chunk + a * cols : q * chunk + a * cols + chunk] for a in range(3)],
+                axis=0,
+            )
+            got = jnp.dot(lhs, rhs, preferred_element_type=jnp.float32)
+            conv_f[q // per_half, :, (q % per_half) * chunk : (q % per_half + 1) * chunk] = got
+            for r in range(chunk_rows):
+                tile = got[:, r * cols : (r + 1) * cols]
+                sums = sums + tile
+                squares = squares + tile * tile
+        turned = jnp.concatenate(
+            [gb[layer, owner] for owner in range(chans)]
+            + [jnp.zeros((C - 8 * chans, cols), jnp.float32)],
+            axis=0,
+        ).T
+        gain = jnp.concatenate(
+            [turned[0:part, 8 * owner : 8 * owner + 1] for owner in range(chans)], axis=0
+        )
+        bias = jnp.concatenate(
+            [turned[0:part, 8 * owner + 1 : 8 * owner + 2] for owner in range(chans)], axis=0
+        )
+        entries = (C // GROUPS) * cells
+        mu = group_sum(sums) / entries
+        var = group_sum(squares) / entries - mu * mu
+        scale = 0.5 * gain / jnp.sqrt(var + 1e-05)
+        return scale, 0.5 * bias - mu * scale
+
+    def acted_of(conv, scale, shift):
+        tiles = []
+        for r in range(chunk_rows):
+            h = conv[:, r * cols : (r + 1) * cols] * scale + shift
+            tiles.append((h + h * jnp.tanh(h)).astype(jnp.bfloat16))
+        return jnp.concatenate(tiles, axis=1)
+
+    forward_field(cond_f, cz_send, cz_recv, cc_send, cc_recv)
+    for row in range(rows):
+        at = (row % per_patch) * cols
+        put_row(cond_f[row // per_patch, :, at : at + cols].astype(jnp.float32), row)
+    forward_layer(0)
+    w_c(0, other).wait_recv()
+
+    for layer in range(sections):
+        last = layer == sections - 1
+        scale, shift = conv_and_stats(layer)
+        if layer == 0:
+            for later in range(1, sections):
+                forward_layer(later)
+            forward_field(noise_f, nz_send, nz_recv, nc_send, nc_recv)
+            for d in steps:
+                f_z(noise_f, nz_send, nz_recv, d, z).wait_send()
+            for owner in range(chans):
+                f_c(noise_f, nc_send, nc_recv, p, owner).wait_send()
+        if not last:
+            for q in range(rows // chunk_rows):
+                where = q // per_half
+                span = slice((q % per_half) * chunk, (q % per_half + 1) * chunk)
+                acted = acted_of(conv_f[where, :, span], scale, shift)
+                out = jnp.dot(weights[layer, 9], acted, preferred_element_type=jnp.float32)
+                before = noise_f[where, :, span].astype(jnp.float32)
+                if layer == 0:
+                    mean = (cond_f[where, :, span].astype(jnp.float32) + out).astype(jnp.bfloat16)
+                    mean_f[where, :, span] = mean
+                    sample = before
+                else:
+                    mean = mean_f[where, :, span]
+                    sample = (before + 0.5 * (out - before)).astype(jnp.bfloat16)
+                    noise_f[where, :, span] = sample
+                    sample = sample.astype(jnp.float32)
+                inputs = (sample + mean.astype(jnp.float32)).astype(jnp.bfloat16).astype(jnp.float32)
+                for r in range(chunk_rows):
+                    put_row(inputs[:, r * cols : (r + 1) * cols], q * chunk_rows + r)
+            w_c(layer + 1, other).wait_recv()
+        else:
+            for q in range(per_half):
+                span = slice(q * chunk, (q + 1) * chunk)
+                acted = acted_of(conv_f[p, :, span], scale, shift)
+                out = jnp.dot(weights[layer, 9, mine, :], acted, preferred_element_type=jnp.float32)
+                before = noise_f[p, mine, span].astype(jnp.float32)
+                sample = (before + 0.5 * (out - before)).astype(jnp.bfloat16).astype(jnp.float32)
+                out_ref[:, span] = (sample + mean_f[p, mine, span].astype(jnp.float32)).astype(
+                    jnp.bfloat16
+                )
+
+    for d in steps:
+        w_z(d, z).wait_send()
+        g_z(d, z).wait_send()
+        f_z(cond_f, cz_send, cz_recv, d, z).wait_send()
+    for d in range(sections - 1):
+        w_s(d, s).wait_send()
+        g_s(d, s).wait_send()
+    for layer in range(sections):
+        w_c(layer, p).wait_send()
+    for owner in range(chans):
+        f_c(cond_f, cc_send, cc_recv, p, owner).wait_send()
+
+
+def fused_body(cond, noise, conv_weight, mix_weight, norm_gain, norm_bias):
+    sections = lax.axis_size("section")
+    chans = lax.axis_size("chan")
+    _, part, own_rows, cols = cond.shape
+    rows = 2 * own_rows
+    own = own_rows * cols
+    gb = jnp.pad(
+        jnp.concatenate([norm_gain, norm_bias], axis=0), ((0, 6), (0, 128 - part))
+    )
+    dma = pltpu.SemaphoreType.DMA
+    near, far = chans - 1, chans
+    out = pl.pallas_call(
+        functools.partial(whole_kernel, sections, chans, rows, cols),
+        out_shape=jax.ShapeDtypeStruct((part, own), jnp.bfloat16),
+        in_specs=[pl.BlockSpec(memory_space=pl.ANY)] * 5,
+        out_specs=pl.BlockSpec(memory_space=pltpu.VMEM),
+        scratch_shapes=[
+            pltpu.VMEM((2, C, own), jnp.bfloat16),
+            pltpu.VMEM((2, C, own), jnp.bfloat16),
+            pltpu.VMEM((2, C, own), jnp.bfloat16),
+            pltpu.VMEM((sections, 10, C, C), jnp.bfloat16),
+            pltpu.VMEM((sections, chans, 8, 128), jnp.float32),
+            pltpu.VMEM((3 * C, (rows + 2) * cols), jnp.bfloat16),
+            pltpu.VMEM((2, C, own), jnp.float32),
+            dma((5,)),
+            dma((near,)), dma((far,)), dma((sections - 1,)), dma((sections,)),
+            dma((sections,)), dma((sections,)),
+            dma((near,)), dma((far,)), dma((sections - 1,)), dma((sections,)),
+            dma((near,)), dma((far,)), dma((far,)), dma((far,)),
+            dma((near,)), dma((far,)), dma((far,)), dma((far,)),
+        ],
+        compiler_params=pltpu.CompilerParams(
+            collective_id=0, has_side_effects=True, vmem_limit_bytes=40 * 1024 * 1024
+        ),
+    )(
+        cond.reshape(part, own), noise.reshape(part, own), conv_weight[0], mix_weight[0], gb
+    )
+    return out.reshape(1, part, own_rows, cols)
+
+
 def solution(mesh):
+    whole = mesh.shape["patch"] == 2
     return jax.shard_map(
-        body,
+        fused_body if whole else body,
         mesh=mesh,
         in_specs=(
             P("section", "chan", "patch", None),

time: 207 us -> 32.4 us (0.16)
  blocking collectives: 145 us -> 0 us
  Pallas kernels: 0 us -> 29.9 us
  waiting for transfers between devices: 18.2 us -> 0 us
  between operations: 13.9 us -> 0.05 us
  starting transfers between devices: 11.4 us -> 0 us
  matrix products: 10.4 us -> 0 us
  other arithmetic: 2.86 us -> 0.01 us
  local copies, waits for them, and re-layouts: 4.77 us -> 2.24 us
    all_gather x8 -> x0, blocking collectives: 117 us -> none  [the longest x4 59.8 us: apply_block(): lax.all_gather(padded, 'chan', axis=1, tiled=True)]
    pallas_call x0 -> x1, Pallas kernels: none -> 29.9 us  [fused_body(): pl.pallas_call(functools.partial(whole_kernel, sections, chans, rows, col...]
    psum x5 -> x0, blocking collectives: 27.6 us -> none  [the longest x1 17.7 us: from_root(): return lax.psum(kept, axis)]
    psum x1 -> x0, waiting for transfers between devices: 13 us -> none  [from_root(): return lax.psum(kept, axis)]
    ppermute x8 -> x0, starting transfers between devices: 11.4 us -> none  [the longest x4 6.23 us: with_halo(): lax.ppermute(tail, axis, [(i, (i + 1) % count) for i in range(ends)])]
    dot_general x40 -> x0, matrix products: 10.4 us -> none  [the longest x36 9.68 us: conv_taps(): jnp.einsum('oc,bchw->bohw', tap_weight[tap_index], window, preferred_elem...]
    ppermute x8 -> x0, waiting for transfers between devices: 5.21 us -> none  [the longest x4 5.2 us: with_halo(): lax.ppermute(head, axis, [((i + 1) % count, i) for i in range(ends)])]
  transfers between devices with their start and end apart: 9 -> 0, of which waited for: 4 -> 0; matrix products, arithmetic and copies ran while one was open for 0% -> 0% of each run, Pallas kernels for 0% -> 0%
where the time goes in v1:
time: 32.4 us; the launch traced here: 32.2 us
  Pallas kernels  29.9 us (92%)
  local copies, waits for them, and re-layouts  2.24 us (7%)
    pallas_call x1, Pallas kernels, fused_body(): pl.pallas_call(functools.partial(whole_kernel, sections, chans, rows, col...  29.9 us
    unnamed x9, local copies, waits for them, and re-layouts  1.32 us
    reshape x1, local copies, waits for them, and re-layouts, fused_body(): noise.reshape(part, own)  0.92 us

profile of v1, /device:TPU:0, one launch (start us, length us, event | category | flops | bytes accessed | tf_op | source)
XLA Modules:
  0.0 32.2 jit_solution(16152346799970283617)
XLA Ops:
  0.0 0.0 copy-start.2
  0.0 0.0 copy-start.3
  0.0 0.7 %copy-done.2 = f32[1,32]{1,0:T(1,128)S(1)} copy-done((f32[1,32]{1,0:T(1,128)S(1)}, f32[1,32]{1,0:T(1,128)}, u32[]{:S(2)}) %copy-start.2) | copy-done | bytes 152
  0.7 0.0 copy-done.3
  0.7 0.0 copy-start
  0.7 0.0 copy-start.1
  0.7 0.9 %copy_bitcast_fusion = (bf16[32,1024]{1,0:T(8,128)(2,1)S(1)}, bf16[32,1024]{1,0:T(8,128)(2,1)S(1)}) fusion(bf16[4,8,8,128]{3,2,1,0:T(8,128)(2,1)} %bitcast.16, bf16[4,8,8,128]{3,2,1,0:T(8,128)(2,1)} %bitcast.17), kind=kLoop, calls=%fused_computation | loop fusion | bytes 262144 | tf_op jit(solution)/shard_map/reshape | solution.py:426
  1.6 0.0 copy-done
  1.6 0.0 copy-done.1
  1.7 29.9 %shard_map.64 = bf16[32,1024]{1,0:T(8,128)(2,1)S(1)} custom-call(bf16[32,1024]{1,0:T(8,128)(2,1)S(1)} %get-tuple-element.6.cond_in, bf16[32,1024]{1,0:T(8,128)(2,1)S(1)} %get-tuple-element.5.noise_in, bf16[9,32,128]{2,1,0:T(8,128)(2,1)S(1)} %bitcast.14, bf16[32,128]{1,0:T(8,128)(2,1)S(1)} %bitcast.15, f32[8,128]{1,0:T(8,128)S(1)} %select_maximum_fusion.gb_in), custom_call_target="tpu_custom_call" | custom-call | tf_op jit(solution)/shard_map/pallas_call | solution.py:402
  31.6 0.6 %copy.9 = bf16[4,8,8,128]{3,2,1,0:T(8,128)(2,1)} copy(bf16[4,8,8,128]{3,1,2,0:T(8,128)(2,1)S(1)} %bitcast.13) | data formatting | bytes 131072
  (1 shorter events, 0.0 us)
Async XLA Ops:
  0.0 0.7 %copy-start.2 = (f32[1,32]{1,0:T(1,128)S(1)}, f32[1,32]{1,0:T(1,128)}, u32[]{:S(2)}) copy-start(f32[1,32]{1,0:T(1,128)} %param.11) | copy-start | bytes 388
  0.0 0.7 %copy-start.3 = (f32[1,32]{1,0:T(1,128)S(1)}, f32[1,32]{1,0:T(1,128)}, u32[]{:S(2)}) copy-start(f32[1,32]{1,0:T(1,128)} %param.10) | copy-start | bytes 388
  0.7 0.9 %copy-start = (bf16[1,9,32,128]{3,2,1,0:T(8,128)(2,1)S(1)}, bf16[1,9,32,128]{3,2,1,0:T(8,128)(2,1)}, u32[]{:S(2)}) copy-start(bf16[1,9,32,128]{3,2,1,0:T(8,128)(2,1)} %param.8) | copy-start | bytes 221188
  0.7 0.9 %copy-start.1 = (bf16[1,32,128]{2,1,0:T(8,128)(2,1)S(1)}, bf16[1,32,128]{2,1,0:T(8,128)(2,1)}, u32[]{:S(2)}) copy-start(bf16[1,32,128]{2,1,0:T(8,128)(2,1)} %param.9) | copy-start | bytes 24580

commit v2 on v1

--- a/solution.py
+++ b/solution.py
@@ -141,16 +141,15 @@
 def whole_kernel(
     sections, chans, rows, cols,
     cond_in, noise_in, conv_in, mix_in, gb_in, out_ref,
-    cond_f, noise_f, mean_f, weights, gb, shifted, conv_f,
+    cond_f, noise_f, mean_f, weights, shifted, conv_f,
     load_sem, wz_send, wz_recv, ws_send, ws_recv, wc_send, wc_recv,
-    gz_send, gz_recv, gs_send, gs_recv,
     cz_send, cz_recv, cc_send, cc_recv, nz_send, nz_recv, nc_send, nc_recv,
 ):
     s = lax.axis_index("section")
     p = lax.axis_index("patch")
     z = lax.axis_index("chan")
     other = 1 - p
-    taps = 10
+    taps = 12
     half = taps // 2
     part = C // chans
     cells = rows * cols
@@ -161,27 +160,29 @@
         return pl.ds(pl.multiple_of(index * part, part), part)
 
     mine = band(z)
-    loads = [
-        pltpu.make_async_copy(
-            conv_in.at[pl.ds(p * half, half - 1)],
-            weights.at[s, pl.ds(p * half, half - 1), mine, :],
-            load_sem.at[0],
-        ),
-        pltpu.make_async_copy(gb_in, gb.at[s, z], load_sem.at[2]),
-        pltpu.make_async_copy(cond_in, cond_f.at[p, mine, :], load_sem.at[3]),
-        pltpu.make_async_copy(noise_in, noise_f.at[p, mine, :], load_sem.at[4]),
-    ]
-    for copy in loads:
-        copy.start()
-    fifth = weights.at[s, p * half + half - 1, mine, :]
+    cond_load = pltpu.make_async_copy(cond_in, cond_f.at[p, mine, :], load_sem.at[0])
+    noise_load = pltpu.make_async_copy(noise_in, noise_f.at[p, mine, :], load_sem.at[1])
+    mix_load = pltpu.make_async_copy(mix_in, weights.at[s, 9, mine, :], load_sem.at[2])
+
+    def conv_load(first, count):
+        return pltpu.make_async_copy(
+            conv_in.at[pl.ds(first, count)],
+            weights.at[s, pl.ds(first, count), mine, :],
+            load_sem.at[3],
+        )
+
+    cond_load.start()
 
     @pl.when(p == 0)
     def _():
-        pltpu.make_async_copy(conv_in.at[half - 1], fifth, load_sem.at[1]).start()
+        conv_load(0, half).start()
 
     @pl.when(p != 0)
     def _():
-        pltpu.make_async_copy(mix_in, fifth, load_sem.at[1]).start()
+        conv_load(half, 9 - half).start()
+        mix_load.start()
+
+    noise_load.start()
 
     barrier = pltpu.get_barrier_semaphore()
     for peer in sec_peers:
@@ -191,75 +192,129 @@
     pl.semaphore_signal(barrier, inc=1, device_id=(s, other, z), device_id_type=MESH)
     pl.semaphore_wait(barrier, sections + chans - 1)
 
+    @pl.when(p == 0)
+    def _():
+        conv_load(0, half).wait()
+
+    @pl.when(p != 0)
+    def _():
+        exact = gb_in[...]
+        high = exact.astype(jnp.bfloat16)
+        rest = exact - high.astype(jnp.float32)
+        middle = rest.astype(jnp.bfloat16)
+        low = (rest - middle.astype(jnp.float32)).astype(jnp.bfloat16)
+        column = lax.broadcasted_iota(jnp.int32, exact.shape, 1)
+        pieces = jnp.where(
+            column < 2,
+            high.astype(jnp.float32),
+            jnp.where(column < 4, middle.astype(jnp.float32), low.astype(jnp.float32)),
+        )
+        weights[s, 10, mine, :] = pieces.astype(jnp.bfloat16)
+        weights[s, 11, mine, :] = jnp.zeros_like(high)
+        conv_load(half, 9 - half).wait()
+        mix_load.wait()
+
     def w_half(layer, which):
         return weights.at[layer, pl.ds(which * half, half)]
 
-    def w_shard(owner):
-        return weights.at[s, pl.ds(p * half, half), band(owner), :]
-
-    def w_z(d, owner):
-        return remote(w_shard(owner), w_shard(owner), wz_send.at[d], wz_recv.at[owner], s, p, z_peers[d])
-
-    def g_z(d, owner):
-        return remote(gb.at[s, owner], gb.at[s, owner], gz_send.at[d], gz_recv.at[owner], s, p, z_peers[d])
-
-    def w_s(d, layer):
-        return remote(w_half(layer, p), w_half(layer, p), ws_send.at[d], ws_recv.at[layer], sec_peers[d], p, z)
-
-    def g_s(d, layer):
-        return remote(gb.at[layer], gb.at[layer], gs_send.at[d], gs_recv.at[layer], sec_peers[d], p, z)
+    def w_shard(layer, owner):
+        return weights.at[layer, pl.ds(p * half, half), band(owner), :]
+
+    def w_z(way, k, owner):
+        block = w_shard(s, owner)
+        return remote(block, block, wz_send.at[way, k], wz_recv.at[owner], s, p, z + 1 - 2 * way)
+
+    def w_s(d, layer, owner):
+        block = w_shard(layer, owner)
+        return remote(block, block, ws_send.at[d, owner], ws_recv.at[layer, owner], sec_peers[d], p, z)
 
     def w_c(layer, which):
         return remote(w_half(layer, which), w_half(layer, which), wc_send.at[layer], wc_recv.at[layer], s, other, z)
 
-    def f_z(field, send, recv, d, owner):
+    def f_z(field, send, recv, way, k, owner):
         block = field.at[p, band(owner), :]
-        return remote(block, block, send.at[d], recv.at[owner], s, p, z_peers[d])
+        return remote(block, block, send.at[way, k], recv.at[owner], s, p, z + 1 - 2 * way)
 
     def f_c(field, send, recv, which, owner):
         block = field.at[which, band(owner), :]
         return remote(block, block, send.at[owner], recv.at[owner], s, other, z)
 
-    steps = range(chans - 1)
-    for copy in loads[:2]:
-        copy.wait()
-    pltpu.make_async_copy(mix_in, fifth, load_sem.at[1]).wait()
-    for d in steps:
-        w_z(d, z).start()
-        g_z(d, z).start()
-    loads[2].wait()
-    for d in steps:
-        f_z(cond_f, cz_send, cz_recv, d, z).start()
-    f_c(cond_f, cc_send, cc_recv, p, z).start()
-    loads[3].wait()
+    cond_z = functools.partial(f_z, cond_f, cz_send, cz_recv)
+    cond_c = functools.partial(f_c, cond_f, cc_send, cc_recv)
+    noise_z = functools.partial(f_z, noise_f, nz_send, nz_recv)
+    noise_c = functools.partial(f_c, noise_f, nc_send, nc_recv)
+
+    def to_sections(owner):
+        for d in range(sections - 1):
+            w_s(d, s, owner).start()
+
+    def along(way, k):
+        owner = z - k if way == 0 else z + k
+        here = z >= k if way == 0 else z + k < chans
+        going = z < chans - 1 if way == 0 else z > 0
+        return owner, here, here & going
+
+    def hop(copy, aside, k):
+        if k == 0:
+            for way in range(2):
+                owner, _, sends = along(way, 0)
+
+                @pl.when(sends)
+                def _():
+                    copy(way, 0, owner).start()
+
+            aside(z)
+            return
+        for way in range(2):
+            owner, here, sends = along(way, k)
+
+            @pl.when(here)
+            def _():
+                copy(way, 0, owner).wait_recv()
+                if k < chans - 1:
+
+                    @pl.when(sends)
+                    def _():
+                        copy(way, k, owner).start()
+
+                aside(owner)
+
+    def sent(copy):
+        for way in range(2):
+            for k in range(chans - 1):
+                owner, _, sends = along(way, k)
+
+                @pl.when(sends)
+                def _():
+                    copy(way, k, owner).wait_send()
+
+    def cond_aside(owner):
+        cond_c(p, owner).start()
+
+    def noise_aside(owner):
+        noise_c(p, owner).start()
+
+    hop(w_z, to_sections, 0)
+    cond_load.wait()
+    hop(cond_z, cond_aside, 0)
+    noise_load.wait()
 
     zero_row = jnp.zeros((3 * C, cols), jnp.bfloat16)
     shifted[:, 0:cols] = zero_row
     shifted[:, (rows + 1) * cols : (rows + 2) * cols] = zero_row
 
-    for d in steps:
-        w_z(d, z_peers[d]).wait_recv()
-        g_z(d, z_peers[d]).wait_recv()
-    for d in range(sections - 1):
-        w_s(d, s).start()
-        g_s(d, s).start()
+    for k in range(1, chans):
+        hop(w_z, to_sections, k)
+        hop(cond_z, cond_aside, k)
+        if k < chans - 1:
+            hop(noise_z, noise_aside, k - 1)
     w_c(s, p).start()
-    for d in steps:
-        f_z(noise_f, nz_send, nz_recv, d, z).start()
-    f_c(noise_f, nc_send, nc_recv, p, z).start()
-
-    def forward_field(field, z_send, z_recv, c_send, c_recv):
-        for d in steps:
-            f_z(field, z_send, z_recv, d, z_peers[d]).wait_recv()
-            f_c(field, c_send, c_recv, p, z_peers[d]).start()
-        for owner in range(chans):
-            f_c(field, c_send, c_recv, other, owner).wait_recv()
 
     def forward_layer(layer):
         @pl.when(s != layer)
         def _():
-            w_s(0, layer).wait_recv()
-            g_s(0, layer).wait_recv()
+            for owner in range(chans):
+                w_s(0, layer, owner).wait_recv()
             w_c(layer, p).start()
 
     lane = lax.broadcasted_iota(jnp.int32, (C, cols), 1)
@@ -302,22 +357,20 @@
                 tile = got[:, r * cols : (r + 1) * cols]
                 sums = sums + tile
                 squares = squares + tile * tile
-        turned = jnp.concatenate(
-            [gb[layer, owner] for owner in range(chans)]
-            + [jnp.zeros((C - 8 * chans, cols), jnp.float32)],
-            axis=0,
-        ).T
-        gain = jnp.concatenate(
-            [turned[0:part, 8 * owner : 8 * owner + 1] for owner in range(chans)], axis=0
-        )
-        bias = jnp.concatenate(
-            [turned[0:part, 8 * owner + 1 : 8 * owner + 2] for owner in range(chans)], axis=0
-        )
+        pieces = weights[layer, 10].astype(jnp.float32)
+        gain = pieces[:, 0:1] + pieces[:, 2:3] + pieces[:, 4:5]
+        bias = pieces[:, 1:2] + pieces[:, 3:4] + pieces[:, 5:6]
         entries = (C // GROUPS) * cells
         mu = group_sum(sums) / entries
         var = group_sum(squares) / entries - mu * mu
         scale = 0.5 * gain / jnp.sqrt(var + 1e-05)
         return scale, 0.5 * bias - mu * scale
+
+    def put_inputs(sample, mean, q):
+        inputs = (sample.astype(jnp.float32) + mean.astype(jnp.float32)).astype(jnp.bfloat16)
+        inputs = inputs.astype(jnp.float32)
+        for r in range(chunk_rows):
+            put_row(inputs[:, r * cols : (r + 1) * cols], q * chunk_rows + r)
 
     def acted_of(conv, scale, shift):
         tiles = []
@@ -326,7 +379,8 @@
             tiles.append((h + h * jnp.tanh(h)).astype(jnp.bfloat16))
         return jnp.concatenate(tiles, axis=1)
 
-    forward_field(cond_f, cz_send, cz_recv, cc_send, cc_recv)
+    for owner in range(chans):
+        cond_c(other, owner).wait_recv()
     for row in range(rows):
         at = (row % per_patch) * cols
         put_row(cond_f[row // per_patch, :, at : at + cols].astype(jnp.float32), row)
@@ -337,32 +391,35 @@
         last = layer == sections - 1
         scale, shift = conv_and_stats(layer)
         if layer == 0:
-            for later in range(1, sections):
-                forward_layer(later)
-            forward_field(noise_f, nz_send, nz_recv, nc_send, nc_recv)
-            for d in steps:
-                f_z(noise_f, nz_send, nz_recv, d, z).wait_send()
-            for owner in range(chans):
-                f_c(noise_f, nc_send, nc_recv, p, owner).wait_send()
+            hop(noise_z, noise_aside, chans - 2)
+            forward_layer(1)
         if not last:
             for q in range(rows // chunk_rows):
                 where = q // per_half
                 span = slice((q % per_half) * chunk, (q % per_half + 1) * chunk)
                 acted = acted_of(conv_f[where, :, span], scale, shift)
                 out = jnp.dot(weights[layer, 9], acted, preferred_element_type=jnp.float32)
+                if layer == 0:
+                    mean = cond_f[where, :, span].astype(jnp.float32) + out
+                    mean_f[where, :, span] = mean.astype(jnp.bfloat16)
+                    continue
                 before = noise_f[where, :, span].astype(jnp.float32)
-                if layer == 0:
-                    mean = (cond_f[where, :, span].astype(jnp.float32) + out).astype(jnp.bfloat16)
-                    mean_f[where, :, span] = mean
-                    sample = before
-                else:
-                    mean = mean_f[where, :, span]
-                    sample = (before + 0.5 * (out - before)).astype(jnp.bfloat16)
-                    noise_f[where, :, span] = sample
-                    sample = sample.astype(jnp.float32)
-                inputs = (sample + mean.astype(jnp.float32)).astype(jnp.bfloat16).astype(jnp.float32)
-                for r in range(chunk_rows):
-                    put_row(inputs[:, r * cols : (r + 1) * cols], q * chunk_rows + r)
+                sample = (before + 0.5 * (out - before)).astype(jnp.bfloat16)
+                noise_f[where, :, span] = sample
+                put_inputs(sample, mean_f[where, :, span], q)
+            if layer == 0:
+                hop(noise_z, noise_aside, chans - 1)
+                for later in range(2, sections):
+                    forward_layer(later)
+                for owner in range(chans):
+                    noise_c(other, owner).wait_recv()
+                for q in range(rows // chunk_rows):
+                    where = q // per_half
+                    span = slice((q % per_half) * chunk, (q % per_half + 1) * chunk)
+                    put_inputs(noise_f[where, :, span], mean_f[where, :, span], q)
+                sent(noise_z)
+                for owner in range(chans):
+                    noise_c(p, owner).wait_send()
             w_c(layer + 1, other).wait_recv()
         else:
             for q in range(per_half):
@@ -375,17 +432,15 @@
                     jnp.bfloat16
                 )
 
-    for d in steps:
-        w_z(d, z).wait_send()
-        g_z(d, z).wait_send()
-        f_z(cond_f, cz_send, cz_recv, d, z).wait_send()
+    sent(w_z)
+    sent(cond_z)
     for d in range(sections - 1):
-        w_s(d, s).wait_send()
-        g_s(d, s).wait_send()
+        for owner in range(chans):
+            w_s(d, s, owner).wait_send()
     for layer in range(sections):
         w_c(layer, p).wait_send()
     for owner in range(chans):
-        f_c(cond_f, cc_send, cc_recv, p, owner).wait_send()
+        cond_c(p, owner).wait_send()
 
 
 def fused_body(cond, noise, conv_weight, mix_weight, norm_gain, norm_bias):
@@ -394,30 +449,27 @@
     _, part, own_rows, cols = cond.shape
     rows = 2 * own_rows
     own = own_rows * cols
-    gb = jnp.pad(
-        jnp.concatenate([norm_gain, norm_bias], axis=0), ((0, 6), (0, 128 - part))
-    )
+    gb = jnp.where(jnp.arange(128)[None, :] % 2 == 0, norm_gain[0][:, None], norm_bias[0][:, None])
     dma = pltpu.SemaphoreType.DMA
     near, far = chans - 1, chans
     out = pl.pallas_call(
         functools.partial(whole_kernel, sections, chans, rows, cols),
         out_shape=jax.ShapeDtypeStruct((part, own), jnp.bfloat16),
-        in_specs=[pl.BlockSpec(memory_space=pl.ANY)] * 5,
+        in_specs=[pl.BlockSpec(memory_space=pl.ANY)] * 4
+        + [pl.BlockSpec(memory_space=pltpu.VMEM)],
         out_specs=pl.BlockSpec(memory_space=pltpu.VMEM),
         scratch_shapes=[
             pltpu.VMEM((2, C, own), jnp.bfloat16),
             pltpu.VMEM((2, C, own), jnp.bfloat16),
             pltpu.VMEM((2, C, own), jnp.bfloat16),
-            pltpu.VMEM((sections, 10, C, C), jnp.bfloat16),
-            pltpu.VMEM((sections, chans, 8, 128), jnp.float32),
+            pltpu.VMEM((sections, 12, C, C), jnp.bfloat16),
             pltpu.VMEM((3 * C, (rows + 2) * cols), jnp.bfloat16),
             pltpu.VMEM((2, C, own), jnp.float32),
-            dma((5,)),
-            dma((near,)), dma((far,)), dma((sections - 1,)), dma((sections,)),
+            dma((4,)),
+            dma((2, near)), dma((far,)), dma((sections - 1, far)), dma((sections, far)),
             dma((sections,)), dma((sections,)),
-            dma((near,)), dma((far,)), dma((sections - 1,)), dma((sections,)),
-            dma((near,)), dma((far,)), dma((far,)), dma((far,)),
-            dma((near,)), dma((far,)), dma((far,)), dma((far,)),
+            dma((2, near)), dma((far,)), dma((far,)), dma((far,)),
+            dma((2, near)), dma((far,)), dma((far,)), dma((far,)),
         ],
         compiler_params=pltpu.CompilerParams(
             collective_id=0, has_side_effects=True, vmem_limit_bytes=40 * 1024 * 1024

time: 32.4 us -> 29.9 us (0.923); the launches traced: 32.2 us -> 29.4 us
  Pallas kernels: 29.9 us -> 27 us
    pallas_call x1, Pallas kernels: 29.9 us -> 27 us  [fused_body(): pl.pallas_call(functools.partial(whole_kernel, sections, chans, rows, col...]
where the time goes in v2:
time: 29.9 us; the launch traced here: 29.4 us
  Pallas kernels  27 us (90%)
  local copies, waits for them, and re-layouts  2.23 us (7%)
    pallas_call x1, Pallas kernels, fused_body(): pl.pallas_call(functools.partial(whole_kernel, sections, chans, rows, col...  27 us
    unnamed x9, local copies, waits for them, and re-layouts  1.31 us
    reshape x1, local copies, waits for them, and re-layouts, fused_body(): noise.reshape(part, own)  0.92 us

profile of v2, /device:TPU:0, one launch (start us, length us, event | category | flops | bytes accessed | tf_op | source)
XLA Modules:
  0.0 29.4 jit_solution(18337340700524593612)
XLA Ops:
  0.0 0.0 copy-start.2
  0.0 0.0 copy-start.3
  0.0 0.6 %copy-done.2 = f32[1,32]{1,0:T(1,128)S(1)} copy-done((f32[1,32]{1,0:T(1,128)S(1)}, f32[1,32]{1,0:T(1,128)}, u32[]{:S(2)}) %copy-start.2) | copy-done | bytes 152
  0.7 0.0 copy-done.3
  0.7 0.1 broadcast_select_fusion.gb_in
  0.7 0.0 copy-start
  0.7 0.0 copy-start.1
  0.7 0.9 %copy_bitcast_fusion = (bf16[32,1024]{1,0:T(8,128)(2,1)S(1)}, bf16[32,1024]{1,0:T(8,128)(2,1)S(1)}) fusion(bf16[4,8,8,128]{3,2,1,0:T(8,128)(2,1)} %bitcast.18, bf16[4,8,8,128]{3,2,1,0:T(8,128)(2,1)} %bitcast.19), kind=kLoop, calls=%fused_computation | loop fusion | bytes 262144 | tf_op jit(solution)/shard_map/reshape | solution.py:478
  1.7 0.0 copy-done
  1.7 0.0 copy-done.1
  1.7 27.0 %shard_map.64 = bf16[32,1024]{1,0:T(8,128)(2,1)S(1)} custom-call(bf16[32,1024]{1,0:T(8,128)(2,1)S(1)} %get-tuple-element.6.cond_in, bf16[32,1024]{1,0:T(8,128)(2,1)S(1)} %get-tuple-element.5.noise_in, bf16[9,32,128]{2,1,0:T(8,128)(2,1)S(1)} %bitcast.16, bf16[32,128]{1,0:T(8,128)(2,1)S(1)} %bitcast.17, f32[32,128]{1,0:T(8,128)S(1)} %broadcast_select_fusion.gb_in), custom_call_target="tpu_custom_call" | custom-call | tf_op jit(solution)/shard_map/pallas_call | solution.py:455
  28.7 0.6 %copy.9 = bf16[4,8,8,128]{3,2,1,0:T(8,128)(2,1)} copy(bf16[4,8,8,128]{3,1,2,0:T(8,128)(2,1)S(1)} %bitcast.15) | data formatting | bytes 131072
  (1 shorter events, 0.0 us)
Async XLA Ops:
  0.0 0.7 %copy-start.2 = (f32[1,32]{1,0:T(1,128)S(1)}, f32[1,32]{1,0:T(1,128)}, u32[]{:S(2)}) copy-start(f32[1,32]{1,0:T(1,128)} %param.11) | copy-start | bytes 388
  0.0 0.7 %copy-start.3 = (f32[1,32]{1,0:T(1,128)S(1)}, f32[1,32]{1,0:T(1,128)}, u32[]{:S(2)}) copy-start(f32[1,32]{1,0:T(1,128)} %param.10) | copy-start | bytes 388
  0.7 0.9 %copy-start = (bf16[1,9,32,128]{3,2,1,0:T(8,128)(2,1)S(1)}, bf16[1,9,32,128]{3,2,1,0:T(8,128)(2,1)}, u32[]{:S(2)}) copy-start(bf16[1,9,32,128]{3,2,1,0:T(8,128)(2,1)} %param.8) | copy-start | bytes 221188
  0.7 0.9 %copy-start.1 = (bf16[1,32,128]{2,1,0:T(8,128)(2,1)S(1)}, bf16[1,32,128]{2,1,0:T(8,128)(2,1)}, u32[]{:S(2)}) copy-start(bf16[1,32,128]{2,1,0:T(8,128)(2,1)} %param.9) | copy-start | bytes 24580

commit v3 on v2

--- a/solution.py
+++ b/solution.py
@@ -141,9 +141,9 @@
 def whole_kernel(
     sections, chans, rows, cols,
     cond_in, noise_in, conv_in, mix_in, gb_in, out_ref,
-    cond_f, noise_f, mean_f, weights, shifted, conv_f,
+    cond_f, noise_f, mean_f, weights, shifted, conv_f, result, landed,
     load_sem, wz_send, wz_recv, ws_send, ws_recv, wc_send, wc_recv,
-    cz_send, cz_recv, cc_send, cc_recv, nz_send, nz_recv, nc_send, nc_recv,
+    cz_send, cz_recv, cc_send, cc_recv, nz_send, nz_recv, nc_send, nc_recv, out_send, out_recv,
 ):
     s = lax.axis_index("section")
     p = lax.axis_index("patch")
@@ -160,6 +160,7 @@
         return pl.ds(pl.multiple_of(index * part, part), part)
 
     mine = band(z)
+    inner = (z > 0) & (z < chans - 1)
     cond_load = pltpu.make_async_copy(cond_in, cond_f.at[p, mine, :], load_sem.at[0])
     noise_load = pltpu.make_async_copy(noise_in, noise_f.at[p, mine, :], load_sem.at[1])
     mix_load = pltpu.make_async_copy(mix_in, weights.at[s, 9, mine, :], load_sem.at[2])
@@ -244,15 +245,28 @@
     noise_z = functools.partial(f_z, noise_f, nz_send, nz_recv)
     noise_c = functools.partial(f_c, noise_f, nc_send, nc_recv)
 
+    pair = pl.ds(pl.multiple_of((z // 2) * 2 * part, 2 * part), 2 * part)
+    chunk_rows = 4
+    chunk = chunk_rows * cols
+    per_half = rows // 2 // chunk_rows
+
+    def give_back(q):
+        span = pl.ds(q * chunk, chunk)
+        away = pl.ds(pl.multiple_of((1 - z % 2) * part, part), part)
+        return remote(
+            result.at[away, span], landed.at[:, span], out_send.at[q], out_recv.at[q],
+            s, p, (z // 2) * (chans - 1),
+        )
+
     def to_sections(owner):
         for d in range(sections - 1):
             w_s(d, s, owner).start()
 
     def along(way, k):
         owner = z - k if way == 0 else z + k
-        here = z >= k if way == 0 else z + k < chans
-        going = z < chans - 1 if way == 0 else z > 0
-        return owner, here, here & going
+        valid = z >= k if way == 0 else z + k < chans
+        going = z < chans - 2 if way == 0 else z > 1
+        return owner, valid & inner, valid & going
 
     def hop(copy, aside, k):
         if k == 0:
@@ -263,7 +277,7 @@
                 def _():
                     copy(way, 0, owner).start()
 
-            aside(z)
+            pl.when(inner)(lambda: aside(z))
             return
         for way in range(2):
             owner, here, sends = along(way, k)
@@ -271,7 +285,7 @@
             @pl.when(here)
             def _():
                 copy(way, 0, owner).wait_recv()
-                if k < chans - 1:
+                if k < chans - 2:
 
                     @pl.when(sends)
                     def _():
@@ -298,149 +312,162 @@
     cond_load.wait()
     hop(cond_z, cond_aside, 0)
     noise_load.wait()
-
-    zero_row = jnp.zeros((3 * C, cols), jnp.bfloat16)
-    shifted[:, 0:cols] = zero_row
-    shifted[:, (rows + 1) * cols : (rows + 2) * cols] = zero_row
-
-    for k in range(1, chans):
-        hop(w_z, to_sections, k)
-        hop(cond_z, cond_aside, k)
-        if k < chans - 1:
-            hop(noise_z, noise_aside, k - 1)
-    w_c(s, p).start()
-
-    def forward_layer(layer):
-        @pl.when(s != layer)
-        def _():
-            for owner in range(chans):
-                w_s(0, layer, owner).wait_recv()
-            w_c(layer, p).start()
-
-    lane = lax.broadcasted_iota(jnp.int32, (C, cols), 1)
-    chan_row = lax.broadcasted_iota(jnp.int32, (C, cols), 0)
-    per_patch = rows // 2
-
-    def put_row(values, row):
-        base = (row + 1) * cols
-        left = jnp.where(lane == 0, 0.0, pltpu.roll(values, 1, 1))
-        right = jnp.where(lane == cols - 1, 0.0, pltpu.roll(values, cols - 1, 1))
-        shifted[0:C, pl.ds(base, cols)] = left.astype(jnp.bfloat16)
-        shifted[C : 2 * C, pl.ds(base, cols)] = values.astype(jnp.bfloat16)
-        shifted[2 * C : 3 * C, pl.ds(base, cols)] = right.astype(jnp.bfloat16)
-
-    def group_sum(values):
-        total = jnp.broadcast_to(jnp.sum(values, axis=1, keepdims=True), (C, cols))
-        for bit in (1, 2):
-            pair = jnp.where(
-                (chan_row // bit) % 2 == 0, pltpu.roll(total, C - bit, 0), pltpu.roll(total, bit, 0)
-            )
-            total = total + pair
-        return total
-
-    chunk_rows = 4
-    chunk = chunk_rows * cols
-    per_half = per_patch // chunk_rows
-
-    def conv_and_stats(layer):
-        lhs = jnp.concatenate([weights[layer, tap] for tap in range(9)], axis=1)
-        sums = jnp.zeros((C, cols), jnp.float32)
-        squares = jnp.zeros((C, cols), jnp.float32)
-        for q in range(rows // chunk_rows):
-            rhs = jnp.concatenate(
-                [shifted[:, q * chunk + a * cols : q * chunk + a * cols + chunk] for a in range(3)],
-                axis=0,
-            )
-            got = jnp.dot(lhs, rhs, preferred_element_type=jnp.float32)
-            conv_f[q // per_half, :, (q % per_half) * chunk : (q % per_half + 1) * chunk] = got
+    hop(noise_z, noise_aside, 0)
+
+    @pl.when(inner)
+    def _():
+        zero_row = jnp.zeros((3 * C, cols), jnp.bfloat16)
+        shifted[:, 0:cols] = zero_row
+        shifted[:, (rows + 1) * cols : (rows + 2) * cols] = zero_row
+
+        for k in range(1, chans - 1):
+            hop(w_z, to_sections, k)
+            hop(cond_z, cond_aside, k)
+            if k < chans - 2:
+                hop(noise_z, noise_aside, k)
+        w_c(s, p).start()
+
+        def forward_layer(layer):
+            @pl.when(s != layer)
+            def _():
+                for owner in range(chans):
+                    w_s(0, layer, owner).wait_recv()
+                w_c(layer, p).start()
+
+        lane = lax.broadcasted_iota(jnp.int32, (C, cols), 1)
+        chan_row = lax.broadcasted_iota(jnp.int32, (C, cols), 0)
+        per_patch = rows // 2
+
+        def put_row(values, row):
+            base = (row + 1) * cols
+            left = jnp.where(lane == 0, 0.0, pltpu.roll(values, 1, 1))
+            right = jnp.where(lane == cols - 1, 0.0, pltpu.roll(values, cols - 1, 1))
+            shifted[0:C, pl.ds(base, cols)] = left.astype(jnp.bfloat16)
+            shifted[C : 2 * C, pl.ds(base, cols)] = values.astype(jnp.bfloat16)
+            shifted[2 * C : 3 * C, pl.ds(base, cols)] = right.astype(jnp.bfloat16)
+
+        def group_sum(values):
+            total = jnp.broadcast_to(jnp.sum(values, axis=1, keepdims=True), (C, cols))
+            for bit in (1, 2):
+                pair = jnp.where(
+                    (chan_row // bit) % 2 == 0, pltpu.roll(total, C - bit, 0), pltpu.roll(total, bit, 0)
+                )
+                total = total + pair
+            return total
+
+        chunk_rows = 4
+        chunk = chunk_rows * cols
+        per_half = per_patch // chunk_rows
+
+        def conv_and_stats(layer):
+            lhs = jnp.concatenate([weights[layer, tap] for tap in range(9)], axis=1)
+            sums = jnp.zeros((C, cols), jnp.float32)
+            squares = jnp.zeros((C, cols), jnp.float32)
+            for q in range(rows // chunk_rows):
+                rhs = jnp.concatenate(
+                    [shifted[:, q * chunk + a * cols : q * chunk + a * cols + chunk] for a in range(3)],
+                    axis=0,
+                )
+                got = jnp.dot(lhs, rhs, preferred_element_type=jnp.float32)
+                conv_f[q // per_half, :, (q % per_half) * chunk : (q % per_half + 1) * chunk] = got
+                for r in range(chunk_rows):
+                    tile = got[:, r * cols : (r + 1) * cols]
+                    sums = sums + tile
+                    squares = squares + tile * tile
+            pieces = weights[layer, 10].astype(jnp.float32)
+            gain = pieces[:, 0:1] + pieces[:, 2:3] + pieces[:, 4:5]
+            bias = pieces[:, 1:2] + pieces[:, 3:4] + pieces[:, 5:6]
+            entries = (C // GROUPS) * cells
+            mu = group_sum(sums) / entries
+            var = group_sum(squares) / entries - mu * mu
+            scale = 0.5 * gain / jnp.sqrt(var + 1e-05)
+            return scale, 0.5 * bias - mu * scale
+
+        def put_inputs(sample, mean, q):
+            inputs = (sample.astype(jnp.float32) + mean.astype(jnp.float32)).astype(jnp.bfloat16)
+            inputs = inputs.astype(jnp.float32)
             for r in range(chunk_rows):
-                tile = got[:, r * cols : (r + 1) * cols]
-                sums = sums + tile
-                squares = squares + tile * tile
-        pieces = weights[layer, 10].astype(jnp.float32)
-        gain = pieces[:, 0:1] + pieces[:, 2:3] + pieces[:, 4:5]
-        bias = pieces[:, 1:2] + pieces[:, 3:4] + pieces[:, 5:6]
-        entries = (C // GROUPS) * cells
-        mu = group_sum(sums) / entries
-        var = group_sum(squares) / entries - mu * mu
-        scale = 0.5 * gain / jnp.sqrt(var + 1e-05)
-        return scale, 0.5 * bias - mu * scale
-
-    def put_inputs(sample, mean, q):
-        inputs = (sample.astype(jnp.float32) + mean.astype(jnp.float32)).astype(jnp.bfloat16)
-        inputs = inputs.astype(jnp.float32)
-        for r in range(chunk_rows):
-            put_row(inputs[:, r * cols : (r + 1) * cols], q * chunk_rows + r)
-
-    def acted_of(conv, scale, shift):
-        tiles = []
-        for r in range(chunk_rows):
-            h = conv[:, r * cols : (r + 1) * cols] * scale + shift
-            tiles.append((h + h * jnp.tanh(h)).astype(jnp.bfloat16))
-        return jnp.concatenate(tiles, axis=1)
-
-    for owner in range(chans):
-        cond_c(other, owner).wait_recv()
-    for row in range(rows):
-        at = (row % per_patch) * cols
-        put_row(cond_f[row // per_patch, :, at : at + cols].astype(jnp.float32), row)
-    forward_layer(0)
-    w_c(0, other).wait_recv()
-
-    for layer in range(sections):
-        last = layer == sections - 1
-        scale, shift = conv_and_stats(layer)
-        if layer == 0:
-            hop(noise_z, noise_aside, chans - 2)
-            forward_layer(1)
-        if not last:
-            for q in range(rows // chunk_rows):
-                where = q // per_half
-                span = slice((q % per_half) * chunk, (q % per_half + 1) * chunk)
-                acted = acted_of(conv_f[where, :, span], scale, shift)
-                out = jnp.dot(weights[layer, 9], acted, preferred_element_type=jnp.float32)
-                if layer == 0:
-                    mean = cond_f[where, :, span].astype(jnp.float32) + out
-                    mean_f[where, :, span] = mean.astype(jnp.bfloat16)
-                    continue
-                before = noise_f[where, :, span].astype(jnp.float32)
-                sample = (before + 0.5 * (out - before)).astype(jnp.bfloat16)
-                noise_f[where, :, span] = sample
-                put_inputs(sample, mean_f[where, :, span], q)
+                put_row(inputs[:, r * cols : (r + 1) * cols], q * chunk_rows + r)
+
+        def acted_of(conv, scale, shift):
+            tiles = []
+            for r in range(chunk_rows):
+                h = conv[:, r * cols : (r + 1) * cols] * scale + shift
+                tiles.append((h + h * jnp.tanh(h)).astype(jnp.bfloat16))
+            return jnp.concatenate(tiles, axis=1)
+
+        for owner in range(chans):
+            cond_c(other, owner).wait_recv()
+        for row in range(rows):
+            at = (row % per_patch) * cols
+            put_row(cond_f[row // per_patch, :, at : at + cols].astype(jnp.float32), row)
+        forward_layer(0)
+        w_c(0, other).wait_recv()
+
+        for layer in range(sections):
+            last = layer == sections - 1
+            scale, shift = conv_and_stats(layer)
             if layer == 0:
-                hop(noise_z, noise_aside, chans - 1)
-                for later in range(2, sections):
-                    forward_layer(later)
-                for owner in range(chans):
-                    noise_c(other, owner).wait_recv()
+                hop(noise_z, noise_aside, chans - 2)
+                forward_layer(1)
+            if not last:
                 for q in range(rows // chunk_rows):
                     where = q // per_half
                     span = slice((q % per_half) * chunk, (q % per_half + 1) * chunk)
-                    put_inputs(noise_f[where, :, span], mean_f[where, :, span], q)
-                sent(noise_z)
-                for owner in range(chans):
-                    noise_c(p, owner).wait_send()
-            w_c(layer + 1, other).wait_recv()
-        else:
-            for q in range(per_half):
-                span = slice(q * chunk, (q + 1) * chunk)
-                acted = acted_of(conv_f[p, :, span], scale, shift)
-                out = jnp.dot(weights[layer, 9, mine, :], acted, preferred_element_type=jnp.float32)
-                before = noise_f[p, mine, span].astype(jnp.float32)
-                sample = (before + 0.5 * (out - before)).astype(jnp.bfloat16).astype(jnp.float32)
-                out_ref[:, span] = (sample + mean_f[p, mine, span].astype(jnp.float32)).astype(
-                    jnp.bfloat16
-                )
+                    acted = acted_of(conv_f[where, :, span], scale, shift)
+                    out = jnp.dot(weights[layer, 9], acted, preferred_element_type=jnp.float32)
+                    if layer == 0:
+                        mean = cond_f[where, :, span].astype(jnp.float32) + out
+                        mean_f[where, :, span] = mean.astype(jnp.bfloat16)
+                        continue
+                    before = noise_f[where, :, span].astype(jnp.float32)
+                    sample = (before + 0.5 * (out - before)).astype(jnp.bfloat16)
+                    noise_f[where, :, span] = sample
+                    put_inputs(sample, mean_f[where, :, span], q)
+                if layer == 0:
+                    for later in range(2, sections):
+                        forward_layer(later)
+                    for owner in range(chans):
+                        noise_c(other, owner).wait_recv()
+                    for q in range(rows // chunk_rows):
+                        where = q // per_half
+                        span = slice((q % per_half) * chunk, (q % per_half + 1) * chunk)
+                        put_inputs(noise_f[where, :, span], mean_f[where, :, span], q)
+                    sent(noise_z)
+                    for owner in range(chans):
+                        noise_c(p, owner).wait_send()
+                w_c(layer + 1, other).wait_recv()
+            else:
+                for q in range(per_half):
+                    span = slice(q * chunk, (q + 1) * chunk)
+                    acted = acted_of(conv_f[p, :, span], scale, shift)
+                    out = jnp.dot(weights[layer, 9, pair, :], acted, preferred_element_type=jnp.float32)
+                    before = noise_f[p, pair, span].astype(jnp.float32)
+                    sample = (before + 0.5 * (out - before)).astype(jnp.bfloat16).astype(jnp.float32)
+                    result[:, span] = (sample + mean_f[p, pair, span].astype(jnp.float32)).astype(
+                        jnp.bfloat16
+                    )
+                    give_back(q).start()
+                    out_ref[:, span] = result[pl.ds(pl.multiple_of((z % 2) * part, part), part), span]
+        for d in range(sections - 1):
+            for owner in range(chans):
+                w_s(d, s, owner).wait_send()
+        for layer in range(sections):
+            w_c(layer, p).wait_send()
+        for owner in range(chans):
+            cond_c(p, owner).wait_send()
+        for q in range(per_half):
+            give_back(q).wait_send()
+
+    @pl.when(jnp.logical_not(inner))
+    def _():
+        sent(noise_z)
+        for q in range(per_half):
+            give_back(q).wait_recv()
+        out_ref[...] = landed[...]
 
     sent(w_z)
     sent(cond_z)
-    for d in range(sections - 1):
-        for owner in range(chans):
-            w_s(d, s, owner).wait_send()
-    for layer in range(sections):
-        w_c(layer, p).wait_send()
-    for owner in range(chans):
-        cond_c(p, owner).wait_send()
 
 
 def fused_body(cond, noise, conv_weight, mix_weight, norm_gain, norm_bias):
@@ -465,11 +492,14 @@
             pltpu.VMEM((sections, 12, C, C), jnp.bfloat16),
             pltpu.VMEM((3 * C, (rows + 2) * cols), jnp.bfloat16),
             pltpu.VMEM((2, C, own), jnp.float32),
+            pltpu.VMEM((2 * part, own), jnp.bfloat16),
+            pltpu.VMEM((part, own), jnp.bfloat16),
             dma((4,)),
             dma((2, near)), dma((far,)), dma((sections - 1, far)), dma((sections, far)),
             dma((sections,)), dma((sections,)),
             dma((2, near)), dma((far,)), dma((far,)), dma((far,)),
             dma((2, near)), dma((far,)), dma((far,)), dma((far,)),
+            dma((2,)), dma((2,)),
         ],
         compiler_params=pltpu.CompilerParams(
             collective_id=0, has_side_effects=True, vmem_limit_bytes=40 * 1024 * 1024
@@ -481,7 +511,7 @@
 
 
 def solution(mesh):
-    whole = mesh.shape["patch"] == 2
+    whole = mesh.shape["patch"] == 2 and mesh.shape["chan"] == 4
     return jax.shard_map(
         fused_body if whole else body,
         mesh=mesh,

time: 29.9 us -> 29.8 us (level)
  the two profiles are of different devices: /device:TPU:0 before, /device:TPU:4 now
where the time goes in v3:
time: 29.8 us; the launch traced here: 29.6 us
  Pallas kernels  27.3 us (92%)
  local copies, waits for them, and re-layouts  2.23 us (7%)
    pallas_call x1, Pallas kernels, fused_body(): pl.pallas_call(functools.partial(whole_kernel, sections, chans, rows, col...  27.3 us
    unnamed x9, local copies, waits for them, and re-layouts  1.31 us
    reshape x1, local copies, waits for them, and re-layouts, fused_body(): noise.reshape(part, own)  0.92 us

profile of v3, /device:TPU:4, one launch (start us, length us, event | category | flops | bytes accessed | tf_op | source)
XLA Modules:
  0.0 29.6 jit_solution(18006263876962327804)
XLA Ops:
  0.0 0.0 copy-start.2
  0.0 0.0 copy-start.3
  0.0 0.6 %copy-done.2 = f32[1,32]{1,0:T(1,128)S(1)} copy-done((f32[1,32]{1,0:T(1,128)S(1)}, f32[1,32]{1,0:T(1,128)}, u32[]{:S(2)}) %copy-start.2) | copy-done | bytes 152
  0.7 0.0 copy-done.3
  0.7 0.1 broadcast_select_fusion.gb_in
  0.7 0.0 copy-start
  0.7 0.0 copy-start.1
  0.7 0.9 %copy_bitcast_fusion = (bf16[32,1024]{1,0:T(8,128)(2,1)S(1)}, bf16[32,1024]{1,0:T(8,128)(2,1)S(1)}) fusion(bf16[4,8,8,128]{3,2,1,0:T(8,128)(2,1)} %bitcast.18, bf16[4,8,8,128]{3,2,1,0:T(8,128)(2,1)} %bitcast.19), kind=kLoop, calls=%fused_computation | loop fusion | bytes 262144 | tf_op jit(solution)/shard_map/reshape | solution.py:508
  1.7 0.0 copy-done
  1.7 0.0 copy-done.1
  1.7 27.3 %shard_map.64 = bf16[32,1024]{1,0:T(8,128)(2,1)S(1)} custom-call(bf16[32,1024]{1,0:T(8,128)(2,1)S(1)} %get-tuple-element.6.cond_in, bf16[32,1024]{1,0:T(8,128)(2,1)S(1)} %get-tuple-element.5.noise_in, bf16[9,32,128]{2,1,0:T(8,128)(2,1)S(1)} %bitcast.16, bf16[32,128]{1,0:T(8,128)(2,1)S(1)} %bitcast.17, f32[32,128]{1,0:T(8,128)S(1)} %broadcast_select_fusion.gb_in), custom_call_target="tpu_custom_call" | custom-call | tf_op jit(solution)/shard_map/pallas_call | solution.py:482
  29.0 0.6 %copy.9 = bf16[4,8,8,128]{3,2,1,0:T(8,128)(2,1)} copy(bf16[4,8,8,128]{3,1,2,0:T(8,128)(2,1)S(1)} %bitcast.15) | data formatting | bytes 131072
  (1 shorter events, 0.0 us)
Async XLA Ops:
  0.0 0.7 %copy-start.2 = (f32[1,32]{1,0:T(1,128)S(1)}, f32[1,32]{1,0:T(1,128)}, u32[]{:S(2)}) copy-start(f32[1,32]{1,0:T(1,128)} %param.11) | copy-start | bytes 388
  0.0 0.7 %copy-start.3 = (f32[1,32]{1,0:T(1,128)S(1)}, f32[1,32]{1,0:T(1,128)}, u32[]{:S(2)}) copy-start(f32[1,32]{1,0:T(1,128)} %param.10) | copy-start | bytes 388
  0.7 0.9 %copy-start = (bf16[1,9,32,128]{3,2,1,0:T(8,128)(2,1)S(1)}, bf16[1,9,32,128]{3,2,1,0:T(8,128)(2,1)}, u32[]{:S(2)}) copy-start(bf16[1,9,32,128]{3,2,1,0:T(8,128)(2,1)} %param.8) | copy-start | bytes 221188
  0.7 0.9 %copy-start.1 = (bf16[1,32,128]{2,1,0:T(8,128)(2,1)S(1)}, bf16[1,32,128]{2,1,0:T(8,128)(2,1)}, u32[]{:S(2)}) copy-start(bf16[1,32,128]{2,1,0:T(8,128)(2,1)} %param.9) | copy-start | bytes 24580

commit v4 on v3

--- a/solution.py
+++ b/solution.py
@@ -154,7 +154,6 @@
     part = C // chans
     cells = rows * cols
     sec_peers = [lax.rem(s + d, sections) for d in range(1, sections)]
-    z_peers = [lax.rem(z + d, chans) for d in range(1, chans)]
 
     def band(index):
         return pl.ds(pl.multiple_of(index * part, part), part)
@@ -186,12 +185,19 @@
     noise_load.start()
 
     barrier = pltpu.get_barrier_semaphore()
-    for peer in sec_peers:
-        pl.semaphore_signal(barrier, inc=1, device_id=(peer, p, z), device_id_type=MESH)
-    for peer in z_peers:
-        pl.semaphore_signal(barrier, inc=1, device_id=(s, p, peer), device_id_type=MESH)
-    pl.semaphore_signal(barrier, inc=1, device_id=(s, other, z), device_id_type=MESH)
-    pl.semaphore_wait(barrier, sections + chans - 1)
+    for step in (-1, 1):
+
+        @pl.when((z + step >= 0) & (z + step < chans))
+        def _():
+            pl.semaphore_signal(barrier, inc=1, device_id=(s, p, z + step), device_id_type=MESH)
+
+    @pl.when(inner)
+    def _():
+        for peer in sec_peers:
+            pl.semaphore_signal(barrier, inc=1, device_id=(peer, p, z), device_id_type=MESH)
+        pl.semaphore_signal(barrier, inc=1, device_id=(s, other, z), device_id_type=MESH)
+
+    pl.semaphore_wait(barrier, jnp.where(inner, sections + 2, 1))
 
     @pl.when(p == 0)
     def _():

time: 29.8 us -> 29.5 us (0.990)
  Pallas kernels: 27.3 us -> 27 us
where the time goes in v4:
time: 29.5 us; the launch traced here: 29.4 us
  Pallas kernels  27 us (92%)
  local copies, waits for them, and re-layouts  2.23 us (8%)
    pallas_call x1, Pallas kernels, fused_body(): pl.pallas_call(functools.partial(whole_kernel, sections, chans, rows, col...  27 us
    unnamed x9, local copies, waits for them, and re-layouts  1.31 us
    reshape x1, local copies, waits for them, and re-layouts, fused_body(): noise.reshape(part, own)  0.92 us

profile of v4, /device:TPU:4, one launch (start us, length us, event | category | flops | bytes accessed | tf_op | source)
XLA Modules:
  0.0 29.4 jit_solution(17916874612144694960)
XLA Ops:
  0.0 0.0 copy-start.2
  0.0 0.0 copy-start.3
  0.0 0.6 %copy-done.2 = f32[1,32]{1,0:T(1,128)S(1)} copy-done((f32[1,32]{1,0:T(1,128)S(1)}, f32[1,32]{1,0:T(1,128)}, u32[]{:S(2)}) %copy-start.2) | copy-done | bytes 152
  0.7 0.0 copy-done.3
  0.7 0.1 broadcast_select_fusion.gb_in
  0.7 0.0 copy-start
  0.7 0.0 copy-start.1
  0.7 0.9 %copy_bitcast_fusion = (bf16[32,1024]{1,0:T(8,128)(2,1)S(1)}, bf16[32,1024]{1,0:T(8,128)(2,1)S(1)}) fusion(bf16[4,8,8,128]{3,2,1,0:T(8,128)(2,1)} %bitcast.18, bf16[4,8,8,128]{3,2,1,0:T(8,128)(2,1)} %bitcast.19), kind=kLoop, calls=%fused_computation | loop fusion | bytes 262144 | tf_op jit(solution)/shard_map/reshape | solution.py:514
  1.7 0.0 copy-done
  1.7 0.0 copy-done.1
  1.7 27.0 %shard_map.64 = bf16[32,1024]{1,0:T(8,128)(2,1)S(1)} custom-call(bf16[32,1024]{1,0:T(8,128)(2,1)S(1)} %get-tuple-element.6.cond_in, bf16[32,1024]{1,0:T(8,128)(2,1)S(1)} %get-tuple-element.5.noise_in, bf16[9,32,128]{2,1,0:T(8,128)(2,1)S(1)} %bitcast.16, bf16[32,128]{1,0:T(8,128)(2,1)S(1)} %bitcast.17, f32[32,128]{1,0:T(8,128)S(1)} %broadcast_select_fusion.gb_in), custom_call_target="tpu_custom_call" | custom-call | tf_op jit(solution)/shard_map/pallas_call | solution.py:488
  28.7 0.6 %copy.9 = bf16[4,8,8,128]{3,2,1,0:T(8,128)(2,1)} copy(bf16[4,8,8,128]{3,1,2,0:T(8,128)(2,1)S(1)} %bitcast.15) | data formatting | bytes 131072
  (1 shorter events, 0.0 us)
Async XLA Ops:
  0.0 0.7 %copy-start.2 = (f32[1,32]{1,0:T(1,128)S(1)}, f32[1,32]{1,0:T(1,128)}, u32[]{:S(2)}) copy-start(f32[1,32]{1,0:T(1,128)} %param.11) | copy-start | bytes 388
  0.0 0.7 %copy-start.3 = (f32[1,32]{1,0:T(1,128)S(1)}, f32[1,32]{1,0:T(1,128)}, u32[]{:S(2)}) copy-start(f32[1,32]{1,0:T(1,128)} %param.10) | copy-start | bytes 388
  0.7 0.9 %copy-start = (bf16[1,9,32,128]{3,2,1,0:T(8,128)(2,1)S(1)}, bf16[1,9,32,128]{3,2,1,0:T(8,128)(2,1)}, u32[]{:S(2)}) copy-start(bf16[1,9,32,128]{3,2,1,0:T(8,128)(2,1)} %param.8) | copy-start | bytes 221188
  0.7 0.9 %copy-start.1 = (bf16[1,32,128]{2,1,0:T(8,128)(2,1)S(1)}, bf16[1,32,128]{2,1,0:T(8,128)(2,1)}, u32[]{:S(2)}) copy-start(bf16[1,32,128]{2,1,0:T(8,128)(2,1)} %param.9) | copy-start | bytes 24580
